TPU v7x, 32 devices: a whole 2x2x4 slice. The times are simulated.
32 devices in a mesh: grp: 4 (over y, x), gx: 4 (over z), gy: 2 (over core).
Axes of the slice: x: 2, y: 2, z: 4, core: 2. Of those that a mesh axis runs over, the one named last changes fastest.
Arguments:
- modes_now: float32 [4, 32, 512, 1024], P('grp', ('gx', 'gy')), may hold values from -6 to 6
- modes_old: float32 [4, 32, 512, 1024], P('grp', ('gx', 'gy')), may hold values from -6 to 6
- pressure_now: float32 [4, 32, 512, 1024], P('grp', None, 'gx', 'gy'), may hold values from -6 to 6
- source: float32 [4, 32, 512, 1024], P('grp', None, 'gx', 'gy'), may hold values from -6 to 6
- strip_slot: int32 [4, 512, 2], P('grp', 'gx', 'gy'), may hold values from 0 to 127, as said below
- strip_row: int32 [4, 512, 2], P('grp', 'gx', 'gy'), may hold values from 0 to 127, as said below
Outputs:
- modes_new: float32 [4, 32, 512, 1024], P('grp', ('gx', 'gy'))
- pressure_next: float32 [4, 32, 512, 1024], P('grp', None, 'gx', 'gy')
Inputs may be any that keep to these rules, and one draw needn't show every extreme that they name: The 128 strips of one device take distinct values of strip_slot. Each device sends to every other device (itself included) either no strip or exactly 4, and every bottom-face strip of every device is met by exactly one top-face strip. `strip_row`: see strip_slot.
All inputs are finite; a program needn't handle non-finite values.
Results may differ from a plain program's by a relative error of at most 0.00007.
Values sent between devices are 32-bit elements; how exact they have to be, the bound alone decides.
A program may use at most 128 MiB of HBM per device.

v0:
```python
import jax
import jax.numpy as jnp
from jax import lax
from jax.sharding import PartitionSpec as P

COURANT = 0.5
WEIGHTS = (1.5, -0.15, 2.0 / 180.0)
HIGH = lax.Precision.HIGHEST


def cosine_table(count):
    rows = jnp.arange(count, dtype=jnp.int32).astype(jnp.float32)[:, None]
    cols = jnp.arange(count, dtype=jnp.int32).astype(jnp.float32)[None, :]
    scale = jnp.where(rows == 0, jnp.sqrt(1.0 / count), jnp.sqrt(2.0 / count))
    return scale * jnp.cos(jnp.pi * rows * (cols + 0.5) / count)


def face_stencil(diff):
    first = diff[..., 0, :]
    second = diff[..., 1, :]
    third = diff[..., 2, :]
    return jnp.stack(
        [
            WEIGHTS[0] * first + WEIGHTS[1] * second + WEIGHTS[2] * third,
            WEIGHTS[1] * first + WEIGHTS[2] * second,
            WEIGHTS[2] * first,
        ],
        axis=-2,
    )


def advance(current, previous, spectrum, depth_index, depth, long_x, long_y):
    index_x = jnp.arange(long_x, dtype=jnp.int32).astype(jnp.float32)
    index_y = jnp.arange(long_y, dtype=jnp.int32).astype(jnp.float32)
    part_z = depth_index / depth * (depth_index / depth)
    part_x = index_x / long_x * (index_x / long_x)
    part_y = index_y / long_y * (index_y / long_y)
    theta = (
        COURANT
        * jnp.pi
        * jnp.sqrt(part_z[:, None, None] + part_x[None, :, None] + part_y[None, None, :])
    )
    shape = jnp.sinc(theta / (2.0 * jnp.pi))
    return 2.0 * jnp.cos(theta) * current - previous + COURANT * COURANT * shape * shape * spectrum


def to_modes(field, table_z, table_x, table_y):
    width_x = lax.axis_size("gx")
    width_y = lax.axis_size("gy")
    depth = field.shape[1]
    planes = depth // (width_x * width_y)
    part = jnp.einsum("kz,gzxy->gkxy", table_z, field, precision=HIGH)
    part = part.reshape(1, width_x, width_y, planes, field.shape[2], field.shape[3])
    part = lax.all_to_all(
        lax.all_to_all(part, "gx", split_axis=1, concat_axis=4, tiled=True),
        "gy",
        split_axis=2,
        concat_axis=5,
        tiled=True,
    )
    part = part.reshape(1, planes, part.shape[4], part.shape[5])
    part = jnp.einsum("kx,gzxy->gzky", table_x, part, precision=HIGH)
    return jnp.einsum("ly,gzky->gzkl", table_y, part, precision=HIGH)


def to_cells(modes, table_z, table_x, table_y):
    width_x = lax.axis_size("gx")
    width_y = lax.axis_size("gy")
    planes = modes.shape[1]
    part = jnp.einsum("ly,gzkl->gzky", table_y, modes, precision=HIGH)
    part = jnp.einsum("kx,gzky->gzxy", table_x, part, precision=HIGH)
    part = part.reshape(1, 1, 1, planes, modes.shape[2], modes.shape[3])
    part = lax.all_to_all(
        lax.all_to_all(part, "gx", split_axis=4, concat_axis=1, tiled=True),
        "gy",
        split_axis=5,
        concat_axis=2,
        tiled=True,
    )
    cells = part.reshape(1, width_x * width_y * planes, part.shape[4], part.shape[5])
    return jnp.einsum("kz,gkxy->gzxy", table_z, cells, precision=HIGH)


def strip_terms(rims, marks, bottom):
    live = marks >= 0
    safe = jnp.where(live, marks, 0)
    met = bottom[safe]
    force = face_stencil(met - rims) * live[..., None, None].astype(jnp.float32)
    return (force, safe)


def shards(modes_now, modes_old, pressure_now, source, strip_slot, strip_row):
    depth = source.shape[1]
    rows_x = source.shape[2]
    cols_y = source.shape[3]
    planes = modes_now.shape[1]
    long_x = modes_now.shape[2]
    long_y = modes_now.shape[3]
    table_z = cosine_table(depth)
    table_x = cosine_table(long_x)
    table_y = cosine_table(long_y)
    top = jnp.stack(
        [pressure_now[0, depth - 1], pressure_now[0, depth - 2], pressure_now[0, depth - 3]], axis=1
    )
    bottom = jnp.transpose(pressure_now[0, 0:3], (1, 0, 2))
    devices = lax.axis_size(("grp", "gx", "gy"))
    slots_per = max(2, rows_x // devices)
    slots = strip_slot.reshape(-1)
    rows = strip_row.reshape(-1)
    buffer = jnp.zeros((devices * slots_per, 3, cols_y), jnp.float32).at[slots].set(top)
    labels = jnp.full((devices * slots_per,), -1, jnp.int32).at[slots].set(rows)
    rims = lax.all_to_all(
        buffer.reshape(devices, slots_per, 3, cols_y),
        ("grp", "gx", "gy"),
        split_axis=0,
        concat_axis=0,
        tiled=True,
    )
    marks = lax.all_to_all(
        labels.reshape(devices, slots_per),
        ("grp", "gx", "gy"),
        split_axis=0,
        concat_axis=0,
        tiled=True,
    )
    force, safe = strip_terms(rims, marks, bottom)
    back = lax.all_to_all(force, ("grp", "gx", "gy"), split_axis=0, concat_axis=0, tiled=True)
    back, force, safe = (back, force, safe)
    top_force = back.reshape(-1, 3, cols_y)[slots]
    bottom_force = (
        jnp.zeros((rows_x, 3, cols_y), jnp.float32)
        .at[safe.reshape(-1)]
        .add(-force.reshape(-1, 3, cols_y))
    )
    forcing = source.at[:, 0:3].add(jnp.transpose(bottom_force, (1, 0, 2))[None])
    forcing = forcing.at[:, depth - 1].add(top_force[:, 0][None])
    forcing = forcing.at[:, depth - 2].add(top_force[:, 1][None])
    forcing = forcing.at[:, depth - 3].add(top_force[:, 2][None])
    spectrum = to_modes(forcing, table_z, table_x, table_y)
    block = lax.axis_index(("gx", "gy"))
    depth_index = (block * planes + jnp.arange(planes, dtype=jnp.int32)).astype(jnp.float32)
    modes_new = advance(
        modes_now[0], modes_old[0], spectrum[0], depth_index, depth, long_x, long_y
    )[None]
    pressure_next = to_cells(modes_new, table_z, table_x, table_y)
    return (modes_new, pressure_next)


def solution(mesh):
    placed = (
        P("grp", ("gx", "gy"), None, None),
        P("grp", ("gx", "gy"), None, None),
        P("grp", None, "gx", "gy"),
        P("grp", None, "gx", "gy"),
        P("grp", "gx", "gy"),
        P("grp", "gx", "gy"),
    )
    return jax.shard_map(
        shards,
        mesh=mesh,
        in_specs=placed,
        out_specs=(P("grp", ("gx", "gy"), None, None), P("grp", None, "gx", "gy")),
        check_vma=False,
    )
```

profile of v0, /device:TPU:9, one launch (start us, length us, event | category | flops | bytes accessed | tf_op | source)
XLA Modules:
  0.0 759.3 jit_solution(17028153232174114819)
XLA Ops:
  0.6 0.7 fusion.69
  1.4 1.1 scatter_custom_fusion
  2.5 0.7 all_to_all.64
  3.2 6.4 all-to-all-start
  9.6 1.2 slice_bitcast_fusion.5
  10.8 0.5 copy.39
  11.5 4.4 scatter_fusion
  15.9 1.2 copy.40
  17.1 5.9 all-to-all-start.1
  23.0 0.5 copy.83
  23.8 1.2 gather_fusion
  25.1 16.8 %all-to-all-done.1 = f32[32,4,3,512]{3,1,2,0:T(4,128)} async-done(((f32[32,4,3,512]{3,1,2,0:T(4,128)}), f32[32,4,3,512]{3,1,2,0:T(4,128)}, u32[]{:S(2)}, u32[]{:S(2)}) %all-to-all-start.1) | async-done | bytes 786464 | tf_op jit(solution)/shard_map/all_to_all | solution.py:112
  41.8 1.6 copy_subtract_fusion
  43.7 1.1 maximum_multiply_fusion.1
  44.8 6.4 all-to-all-start.2
  51.2 10.9 %copy.45 = f32[1,32,128,512]{3,0,2,1:T(1,128)} copy(f32[1,32,128,512]{3,2,1,0:T(8,128)} %param.17) | data formatting | bytes 16777216 | tf_op args[3]
  62.1 0.5 broadcast.410
  62.6 0.6 reduce.15
  64.6 0.8 fusion.38
  65.6 5.8 scatter_fusion.1
  71.4 0.7 copy_add_fusion
  72.1 1.7 copy_dynamic-update-slice_fusion
  73.8 1.6 copy.49
  75.3 1.2 gather_fusion.1
  76.5 1.9 fusion.54
  78.4 2.1 fusion.52
  80.5 1.4 fusion.56
  81.9 4.7 copy.82
  86.6 15.2 %fusion.23 = f32[1,32,128,512]{3,1,2,0:T(8,128)S(1)} fusion(f32[32,128,512]{2,1,0:T(8,128)S(1)} %copy_dynamic-update-slice_fusion.1, f32[32]{0:T(128)S(1)} %get-tuple-element.63, f32[32]{0:T(128)S(1)} %convert_multiply_fusion.2, f32[32]{0:T(128)S(1)} %get-tuple-element.62), kind=kOutput, calls=%fused_computation.43 | convolution fusion | flops 805309440 | bytes 16777600 | tf_op jit(solution)/shard_map/kz,gzxy->gkxy/dot_general | solution.py:52
  101.8 8.3 %copy.68 = f32[1,32,128,512]{3,2,1,0:T(8,128)} copy(f32[1,32,128,512]{3,1,2,0:T(8,128)S(1)} %fusion.23) | data formatting | bytes 16777216 | tf_op jit(solution)/shard_map/reshape | solution.py:53
  110.1 5.8 all-to-all-start.3
  116.1 15.5 %fusion.86 = f32[1024,1024,1]{1,0,2:T(8,128)} fusion(f32[1024]{0:T(1024)S(1)} %get-tuple-element.67, f32[1024]{0:T(1024)S(1)} %get-tuple-element.68, f32[1024]{0:T(1024)S(1)} %get-tuple-element.69), kind=kLoop, calls=%fused_computation.40.clone.clone.clone.1 | loop fusion | flops 3145728 | bytes 4206592 | tf_op jit(solution)/shard_map/ly,gzky->gzkl/dot_general | solution.py:63
  131.6 164.0 %all-to-all-done.3 = f32[1,4,2,4,128,512]{5,4,3,2,0,1:T(8,128)} async-done(((f32[1,4,2,4,128,512]{5,4,3,2,0,1:T(8,128)}), f32[1,4,2,4,128,512]{5,4,3,2,0,1:T(8,128)}, u32[]{:S(2)}, u32[]{:S(2)}) %all-to-all-start.3) | async-done | bytes 8388640 | tf_op jit(solution)/shard_map/all_to_all | solution.py:55
  295.6 4.4 copy.54
  299.9 12.7 %all_to_all.91 = f32[1,1,2,4,512,512]{5,4,3,1,0,2:T(8,128)} all-to-all(f32[1,1,2,4,512,512]{5,4,3,1,0,2:T(8,128)S(1)} %bitcast.142), channel_id=1, replica_groups=mesh['grp'=4,'gx'=4,'gy'=2] {'gy'}, dimensions={2} | all-to-all | bytes 16777216 | tf_op jit(solution)/shard_map/all_to_all | solution.py:54
  312.6 9.9 %copy.56 = f32[1,1,1,4,512,2,512]{4,6,5,3,2,1,0:T(8,128)} copy(f32[1,1,1,4,512,2,512]{6,4,3,5,2,1,0:T(8,128)} %bitcast.143) | data formatting | bytes 16777216 | tf_op jit(solution)/shard_map/all_to_all | solution.py:54
  322.5 24.1 %fusion.40 = f32[4,1024,512]{2,1,0:T(8,128)S(1)} fusion(f32[4,512,1024]{1,2,0:T(8,128)} %bitcast.140, f32[512]{0:T(512)S(1)} %get-tuple-element.64, f32[512]{0:T(512)S(1)} %get-tuple-element.65, f32[512]{0:T(512)S(1)} %fusion.68), kind=kOutput, calls=%fused_computation.58 | convolution fusion | flops 12885688320 | bytes 16783360 | tf_op jit(solution)/shard_map/kx,gzxy->gzky/dot_general | solution.py:62
  346.6 70.8 %fusion.9 = f32[1,4,512,1024]{3,2,1,0:T(8,128)S(1)} fusion(f32[1,4,512,1024]{3,2,1,0:T(8,128)} %param.15, f32[1,4,512,1024]{3,2,1,0:T(8,128)} %param.14, f32[1024]{0:T(1024)S(1)} %get-tuple-element.66, f32[4,512]{1,0:T(4,128)S(1)} %broadcast_add_fusion, f32[4,1024,512]{2,1,0:T(8,128)S(1)} %fusion.40, f32[1024,1024,1]{1,0,2:T(8,128)S(1)} %copy-done), kind=kOutput, calls=%fused_computation.21 | convolution fusion | flops 25862078464 | bytes 37761024 | tf_op jit(solution)/shard_map/ly,gzky->gzkl/dot_general | solution.py:63
  417.5 45.8 %fusion.12 = f32[4,512,1024]{1,2,0:T(8,128)S(1)} fusion(f32[1,4,512,1024]{3,2,1,0:T(8,128)S(1)} %fusion.9, f32[1024]{0:T(1024)S(1)} %get-tuple-element.67, f32[1024]{0:T(1024)S(1)} %get-tuple-element.68, f32[1024]{0:T(1024)S(1)} %get-tuple-element.69), kind=kOutput, calls=%fused_computation.25 | convolution fusion | flops 25772949504 | bytes 16789504 | tf_op jit(solution)/shard_map/ly,gzkl->gzky/dot_general | solution.py:70
  463.3 23.2 %convolution_bitcast_fusion = f32[1,1,1,4,512,1024]{4,5,3,2,1,0:T(8,128)} fusion(f32[4,512,1024]{1,2,0:T(8,128)S(1)} %fusion.12, f32[512]{0:T(512)S(1)} %get-tuple-element.64, f32[512]{0:T(512)S(1)} %get-tuple-element.65, f32[512]{0:T(512)S(1)} %fusion.68), kind=kOutput, calls=%fused_computation.42 | convolution fusion | flops 12885688320 | bytes 16783360 | tf_op jit(solution)/shard_map/kx,gzky->gzxy/dot_general | solution.py:71
  486.5 10.5 %copy.59 = f32[1,1,1,4,512,1024]{5,3,2,1,0,4:T(4,128)} copy(f32[1,1,1,4,512,1024]{4,5,3,2,1,0:T(8,128)} %convolution_bitcast_fusion) | data formatting | bytes 16777216 | tf_op jit(solution)/shard_map/reshape | solution.py:72
  497.0 191.5 %all_to_all.92 = f32[1,1,1,4,512,1024]{5,3,2,1,0,4:T(4,128)} all-to-all(f32[1,1,1,4,512,1024]{5,3,2,1,0,4:T(4,128)} %copy.59), channel_id=1, replica_groups=mesh['grp'=4,'gx'=4,'gy'=2] {'gx'}, dimensions={4} | all-to-all | bytes 16777216 | tf_op jit(solution)/shard_map/all_to_all | solution.py:74
  688.5 10.3 %copy.60 = f32[1,1,1,4,4,128,1024]{5,4,3,6,2,1,0:T(4,128)} copy(f32[1,1,1,4,4,128,1024]{6,3,5,4,2,1,0:T(4,128)} %bitcast.144) | data formatting | bytes 16777216 | tf_op jit(solution)/shard_map/all_to_all | solution.py:74
  698.8 19.9 %all_to_all.93 = f32[1,4,1,4,128,1024]{4,1,3,2,0,5:T(4,128)} all-to-all(f32[1,4,1,4,128,1024]{4,1,3,2,0,5:T(4,128)} %bitcast.145), channel_id=1, replica_groups=mesh['grp'=4,'gx'=4,'gy'=2] {'gy'}, dimensions={5} | all-to-all | bytes 16777216 | tf_op jit(solution)/shard_map/all_to_all | solution.py:73
  718.7 10.7 %copy.61 = f32[1,4,1,4,128,2,512]{6,3,5,1,4,2,0:T(4,128)} copy(f32[1,4,1,4,128,2,512]{4,1,3,6,5,2,0:T(4,128)} %bitcast.146) | data formatting | bytes 16777216 | tf_op jit(solution)/shard_map/all_to_all | solution.py:73
  729.4 10.0 %reshape.483 = f32[32,128,512]{2,0,1:T(8,128)} reshape(f32[1,4,2,1,4,128,512]{6,4,2,1,5,3,0:T(4,128)} %bitcast.147) | data formatting | bytes 16777216 | tf_op jit(solution)/shard_map/reshape.162
  739.4 11.2 %convolution_bitcast_fusion.1 = f32[1,32,128,512]{3,1,2,0:T(8,128)S(1)} fusion(f32[32,128,512]{2,0,1:T(8,128)} %reshape.483, f32[32]{0:T(128)S(1)} %get-tuple-element.63, f32[32]{0:T(128)S(1)} %convert_multiply_fusion.2, f32[32]{0:T(128)S(1)} %get-tuple-element.62), kind=kOutput, calls=%fused_computation.44 | convolution fusion | flops 805309440 | bytes 16777600 | tf_op jit(solution)/shard_map/kz,gkxy->gzxy/dot_general | solution.py:81
  750.6 8.3 %copy.62 = f32[1,32,128,512]{3,2,1,0:T(8,128)} copy(f32[1,32,128,512]{3,1,2,0:T(8,128)S(1)} %convolution_bitcast_fusion.1) | data formatting | bytes 16777216
  (38 shorter events, 2.4 us)
Async XLA Ops:
  0.6 22.3 %slice-start.1 = ((f32[1,32,128,512]{3,2,1,0:T(8,128)}), f32[1,3,128,512]{3,2,1,0:T(8,128)S(1)}, s32[]{:S(2)}) async-start(f32[1,32,128,512]{3,2,1,0:T(8,128)} %param.16), calls=%async_computation.8 | async-start | bytes 1572864 | tf_op jit(solution)/shard_map/slice | solution.py:105
  3.2 13.9 %all-to-all-start = ((s32[32,1,4]{2,1,0:T(1,128)}), s32[32,1,4]{2,1,0:T(1,128)S(1)}, u32[]{:S(2)}, u32[]{:S(2)}) async-start(s32[32,1,4]{2,1,0:T(1,128)} %bitcast.3), calls=%async_computation | async-start | bytes 32768 | tf_op jit(solution)/shard_map/all_to_all | solution.py:119
  17.1 24.7 %all-to-all-start.1 = ((f32[32,4,3,512]{3,1,2,0:T(4,128)}), f32[32,4,3,512]{3,1,2,0:T(4,128)}, u32[]{:S(2)}, u32[]{:S(2)}) async-start(f32[32,4,3,512]{3,1,2,0:T(4,128)} %copy.40), calls=%async_computation.1 | async-start | bytes 1572864 | tf_op jit(solution)/shard_map/all_to_all | solution.py:112
  44.8 29.0 %all-to-all-start.2 = ((f32[32,4,3,512]{3,1,2,0:T(4,128)}), f32[32,4,3,512]{3,1,2,0:T(4,128)}, u32[]{:S(2)}, u32[]{:S(2)}) async-start(f32[32,4,3,512]{3,1,2,0:T(4,128)} %maximum_multiply_fusion.1), calls=%async_computation.2 | async-start | bytes 1572864 | tf_op jit(solution)/shard_map/all_to_all | solution.py:127
  51.2 20.2 %slice-start = ((f32[1,32,128,512]{3,2,1,0:T(8,128)}), f32[1,3,128,512]{3,2,1,0:T(8,128)S(1)}, s32[]{:S(2)}) async-start(f32[1,32,128,512]{3,2,1,0:T(8,128)} %param.17), calls=%async_computation.7 | async-start | bytes 1572864 | tf_op jit(solution)/shard_map/slice.108
  110.1 185.5 %all-to-all-start.3 = ((f32[1,4,2,4,128,512]{5,4,3,2,0,1:T(8,128)}), f32[1,4,2,4,128,512]{5,4,3,2,0,1:T(8,128)}, u32[]{:S(2)}, u32[]{:S(2)}) async-start(f32[1,4,2,4,128,512]{5,4,3,2,0,1:T(8,128)} %bitcast.141), calls=%async_computation.3 | async-start | bytes 16777216 | tf_op jit(solution)/shard_map/all_to_all | solution.py:55
  322.5 24.1 %copy-start = (f32[1024,1024,1]{1,0,2:T(8,128)S(1)}, f32[1024,1024,1]{1,0,2:T(8,128)}, u32[]{:S(2)}) copy-start(f32[1024,1024,1]{1,0,2:T(8,128)} %fusion.86) | copy-start | bytes 12582916
  417.5 45.9 %copy-start.1 = (f32[1,4,512,1024]{3,2,1,0:T(8,128)}, f32[1,4,512,1024]{3,2,1,0:T(8,128)S(1)}, u32[]{:S(2)}) copy-start(f32[1,4,512,1024]{3,2,1,0:T(8,128)S(1)} %fusion.9) | copy-start | bytes 25165828
where the time goes:
time: 770 us; the launch traced here: 759 us
  blocking collectives  224 us (29%)
  matrix products  190 us (25%)
  waiting for transfers between devices  181 us (24%)
  local copies, waits for them, and re-layouts  105 us (14%)
  other arithmetic  32.7 us (4%)
  starting transfers between devices  24.4 us (3%)
    all_to_all x1, blocking collectives, to_cells(): lax.all_to_all(part, 'gx', split_axis=4, concat_axis=1, tiled=True)  192 us
    all_to_all x1, waiting for transfers between devices, to_modes(): lax.all_to_all(part, 'gx', split_axis=1, concat_axis=4, tiled=True)  164 us
    dot_general x1, matrix products, to_modes(): return jnp.einsum('ly,gzky->gzkl', table_y, part, precision=HIGH)  70.8 us
    dot_general x1, matrix products, to_cells(): part = jnp.einsum('ly,gzkl->gzky', table_y, modes, precision=HIGH)  45.8 us
    unnamed x8, local copies, waits for them, and re-layouts  24.5 us
    dot_general x1, matrix products, to_modes(): part = jnp.einsum('kx,gzxy->gzky', table_x, part, precision=HIGH)  24.1 us
    dot_general x1, matrix products, to_cells(): part = jnp.einsum('kx,gzky->gzxy', table_x, part, precision=HIGH)  23.2 us
    all_to_all x1, blocking collectives, to_cells(): lax.all_to_all(lax.all_to_all(part, 'gx', split_axis=4, concat_axis=1, ti...  19.9 us
  transfers between devices with their start and end apart: 4, of which 2 were waited for; matrix products, arithmetic and copies ran while one was open for 6% of the time, Pallas kernels for 0%

commit v1 on v0

v1 whole, which is shorter than its diff:
```python
import functools

import jax
import jax.numpy as jnp
import ml_dtypes
import numpy as np
from jax import lax
from jax.experimental import pallas as pl
from jax.experimental.pallas import tpu as pltpu
from jax.sharding import PartitionSpec as P

COURANT = 0.5
WEIGHTS = (1.5, -0.15, 2.0 / 180.0)
HIGH = lax.Precision.HIGHEST


def cosine_table(count):
    rows = np.arange(count, dtype=np.float32)[:, None]
    cols = np.arange(count, dtype=np.float32)[None, :]
    angle = (np.float32(np.pi) * rows) * (cols + np.float32(0.5)) / np.float32(count)
    scale = np.where(rows == 0, np.float32(np.sqrt(1.0 / count)), np.float32(np.sqrt(2.0 / count)))
    return (scale * np.cos(angle.astype(np.float64)).astype(np.float32)).astype(np.float32)


def halves(table):
    high = table.astype(ml_dtypes.bfloat16)
    low = (table - high.astype(np.float32)).astype(ml_dtypes.bfloat16)
    return np.stack([high, low])


def split(block):
    high = block.astype(jnp.bfloat16)
    return high, (block - high.astype(jnp.float32)).astype(jnp.bfloat16)


def dot3(left, right):
    def dot(a, b):
        return jnp.dot(a, b, preferred_element_type=jnp.float32)

    return dot(left[0], right[0]) + (dot(left[0], right[1]) + dot(left[1], right[0]))


def face_stencil(diff):
    first = diff[..., 0, :]
    second = diff[..., 1, :]
    third = diff[..., 2, :]
    return jnp.stack(
        [
            WEIGHTS[0] * first + WEIGHTS[1] * second + WEIGHTS[2] * third,
            WEIGHTS[1] * first + WEIGHTS[2] * second,
            WEIGHTS[2] * first,
        ],
        axis=-2,
    )


SERIES = tuple(float((-1) ** k * 2.0 ** (2 * k + 1) / np.prod(np.arange(1.0, 2 * k + 3))) for k in range(11))


def middle(
    n_gx, n_gy, part, now, old, cx, cxt, cy, cyt, modes, cells,
    recv, mid, back, out, now_v, old_v, new_v,
    f_send, f_recv, i_send, i_recv, own_f, own_i, load, store,
):
    n = n_gx * n_gy
    planes, long_x, long_y = recv.shape
    rows_x, cols_y = part.shape[1:]
    gx = lax.axis_index("gx")
    gy = lax.axis_index("gy")
    me = gx * n_gy + gy

    def peer(k):
        other = lax.rem(me + k, n)
        return other, lax.div(other, n_gy), lax.rem(other, n_gy)

    def block(x, y):
        return (
            pl.ds(pl.multiple_of(x * rows_x, rows_x), rows_x),
            pl.ds(pl.multiple_of(y * cols_y, cols_y), cols_y),
        )

    here = block(gx, gy)

    def forward(p, k):
        other, x, y = peer(k)
        return pltpu.make_async_remote_copy(
            src_ref=part.at[other * planes + p],
            dst_ref=recv.at[(p,) + here],
            send_sem=f_send.at[p, k],
            recv_sem=f_recv.at[p, k],
            device_id={"gx": x, "gy": y},
            device_id_type=pl.DeviceIdType.MESH,
        )

    def inverse(p, k):
        other, x, y = peer(k)
        return pltpu.make_async_remote_copy(
            src_ref=out.at[(p,) + block(x, y)],
            dst_ref=cells.at[me * planes + p],
            send_sem=i_send.at[p, k],
            recv_sem=i_recv.at[p, k],
            device_id={"gx": x, "gy": y},
            device_id_type=pl.DeviceIdType.MESH,
        )

    def own_forward(p):
        return pltpu.make_async_copy(part.at[me * planes + p], recv.at[(p,) + here], own_f.at[p])

    def own_inverse(p):
        return pltpu.make_async_copy(out.at[(p,) + here], cells.at[me * planes + p], own_i.at[p])

    def start_forward(p):
        own_forward(p).start()
        for k in range(1, n):
            forward(p, k).start()

    barrier = pltpu.get_barrier_semaphore()
    for k in range(1, n):
        other, x, y = peer(k)
        pl.semaphore_signal(
            barrier, inc=1, device_id={"gx": x, "gy": y}, device_id_type=pl.DeviceIdType.MESH
        )
    pl.semaphore_wait(barrier, n - 1)

    for p in range(min(2, planes)):
        start_forward(p)
    wide = 256
    tall = 128
    for p in range(planes):
        get_now = pltpu.make_async_copy(now.at[p], now_v, load.at[0])
        get_old = pltpu.make_async_copy(old.at[p], old_v, load.at[1])
        get_now.start()
        get_old.start()
        own_forward(p).wait()
        for k in range(1, n):
            forward(p, k).wait_recv()
        if p + 2 < planes:
            start_forward(p + 2)

        @pl.loop(0, long_y // wide)
        def _(j):
            cols = pl.ds(pl.multiple_of(j * wide, wide), wide)
            mid[:, cols] = dot3((cx[0], cx[1]), split(recv[p, :, cols]))

        get_now.wait()
        get_old.wait()
        depth = n * planes
        at_z = (me * planes + p).astype(jnp.float32) / depth

        @pl.loop(0, long_x // tall)
        def _(i):
            rows = pl.ds(pl.multiple_of(i * tall, tall), tall)
            spectrum = dot3(split(mid[rows, :]), (cyt[0], cyt[1]))
            at_x = (i * tall + lax.broadcasted_iota(jnp.int32, (tall, 1), 0)).astype(
                jnp.float32
            ) / long_x
            at_y = lax.broadcasted_iota(jnp.int32, (1, long_y), 1).astype(jnp.float32) / long_y
            half = (COURANT * np.pi / 2.0) ** 2
            u = half * (at_z * at_z + at_x * at_x + at_y * at_y)
            shape = jnp.full((tall, long_y), SERIES[-1], jnp.float32)
            for term in SERIES[-2::-1]:
                shape = shape * u + term
            new = (
                (2.0 - 4.0 * (u * shape)) * now_v[rows, :]
                - old_v[rows, :]
                + (COURANT * COURANT) * shape * spectrum
            )
            new_v[rows, :] = new
            back[rows, :] = dot3(split(new), (cy[0], cy[1]))

        put = pltpu.make_async_copy(new_v, modes.at[p], store.at[0])
        put.start()

        @pl.loop(0, long_y // wide)
        def _(j):
            cols = pl.ds(pl.multiple_of(j * wide, wide), wide)
            out[p, :, cols] = dot3((cxt[0], cxt[1]), split(back[:, cols]))

        own_inverse(p).start()
        for k in range(1, n):
            inverse(p, k).start()
        put.wait()
    for p in range(planes):
        own_inverse(p).wait()
        for k in range(1, n):
            forward(p, k).wait_send()
            inverse(p, k).wait()


def through_modes(part, now, old, table_x, table_y):
    n_gx = lax.axis_size("gx")
    n_gy = lax.axis_size("gy")
    n = n_gx * n_gy
    planes, long_x, long_y = now.shape
    plane = pltpu.VMEM((long_x, long_y), jnp.float32)
    stack = pltpu.VMEM((planes, long_x, long_y), jnp.float32)
    sems = pltpu.SemaphoreType.DMA((planes, n))
    hbm = pl.BlockSpec(memory_space=pl.ANY)
    vmem = pl.BlockSpec(memory_space=pltpu.VMEM)
    return pl.pallas_call(
        functools.partial(middle, n_gx, n_gy),
        out_shape=(
            jax.ShapeDtypeStruct(now.shape, jnp.float32),
            jax.ShapeDtypeStruct(part.shape, jnp.float32),
        ),
        in_specs=[hbm] * 3 + [vmem] * 4,
        out_specs=(hbm, hbm),
        scratch_shapes=[
            stack, plane, plane, stack, plane, plane, plane,
            sems, sems, sems, sems,
            pltpu.SemaphoreType.DMA((planes,)),
            pltpu.SemaphoreType.DMA((planes,)),
            pltpu.SemaphoreType.DMA((2,)),
            pltpu.SemaphoreType.DMA((1,)),
        ],
        compiler_params=pltpu.CompilerParams(
            collective_id=0, has_side_effects=True, vmem_limit_bytes=56 * 2**20
        ),
        cost_estimate=pl.CostEstimate(
            flops=12 * planes * long_x * long_y * (long_x + long_y),
            bytes_accessed=24 * planes * long_x * long_y,
            transcendentals=0,
        ),
        name="middle",
    )(
        part,
        now,
        old,
        jnp.asarray(halves(table_x)),
        jnp.asarray(halves(table_x.T)),
        jnp.asarray(halves(table_y)),
        jnp.asarray(halves(table_y.T)),
    )


def swap(strips, devices):
    return lax.all_to_all(
        strips.reshape(devices, -1, strips.shape[1]),
        ("grp", "gx", "gy"),
        split_axis=0,
        concat_axis=0,
        tiled=True,
    ).reshape(strips.shape)


def shards(modes_now, modes_old, pressure_now, source, strip_slot, strip_row):
    depth = source.shape[1]
    rows_x = source.shape[2]
    cols_y = source.shape[3]
    long_x = modes_now.shape[2]
    long_y = modes_now.shape[3]
    table_z = jnp.asarray(cosine_table(depth))
    table_x = cosine_table(long_x)
    table_y = cosine_table(long_y)
    layers = pressure_now[0]
    top = jnp.transpose(layers[depth - 3 :][::-1], (1, 0, 2)).reshape(rows_x, 3 * cols_y)
    bottom = jnp.transpose(layers[0:3], (1, 0, 2)).reshape(rows_x, 3 * cols_y)
    devices = lax.axis_size(("grp", "gx", "gy"))
    slots_per = max(2, rows_x // devices)
    slots = strip_slot.reshape(-1)
    rows = strip_row.reshape(-1)
    places = jnp.arange(devices * slots_per, dtype=jnp.int32)
    put = (places[:, None] == slots[None, :]).astype(jnp.float32)
    label = jnp.broadcast_to((rows + 1).astype(jnp.float32)[:, None], (rows_x, 128))
    sent = jnp.dot(put, jnp.concatenate([top, label], axis=1), precision=HIGH)
    rims = swap(sent, devices)
    marks = rims[:, 3 * cols_y].astype(jnp.int32) - 1
    meet = (marks[:, None] == jnp.arange(rows_x, dtype=jnp.int32)[None, :]).astype(jnp.float32)
    met = jnp.dot(meet, bottom, precision=HIGH)
    diff = (met - rims[:, : 3 * cols_y]).reshape(-1, 3, cols_y)
    force = face_stencil(diff).reshape(-1, 3 * cols_y)
    back = swap(force, devices)
    bottom_force = -jnp.dot(meet.T, force, precision=HIGH).reshape(rows_x, 3, cols_y)
    top_force = jnp.dot(put.T, back, precision=HIGH).reshape(rows_x, 3, cols_y)
    forcing = source.at[0, 0:3].add(jnp.transpose(bottom_force, (1, 0, 2)))
    forcing = forcing.at[0, depth - 3 :].add(jnp.transpose(top_force, (1, 0, 2))[::-1])
    part = jnp.einsum("kz,zxy->kxy", table_z, forcing[0], precision=lax.Precision.HIGH)
    modes_new, cells = through_modes(part, modes_now[0], modes_old[0], table_x, table_y)
    pressure_next = jnp.einsum("kz,kxy->zxy", table_z, cells, precision=lax.Precision.HIGH)
    return (modes_new[None], pressure_next[None])


def solution(mesh):
    placed = (
        P("grp", ("gx", "gy"), None, None),
        P("grp", ("gx", "gy"), None, None),
        P("grp", None, "gx", "gy"),
        P("grp", None, "gx", "gy"),
        P("grp", "gx", "gy"),
        P("grp", "gx", "gy"),
    )
    return jax.shard_map(
        shards,
        mesh=mesh,
        in_specs=placed,
        out_specs=(P("grp", ("gx", "gy"), None, None), P("grp", None, "gx", "gy")),
        check_vma=False,
    )
```

time: 770 us -> 493 us (0.64)
  Pallas kernels: 0 us -> 371 us
  blocking collectives: 224 us -> 0 us
  matrix products: 190 us -> 29.6 us
  waiting for transfers between devices: 181 us -> 26.2 us
  local copies, waits for them, and re-layouts: 105 us -> 43.7 us
  other arithmetic: 32.7 us -> 4.47 us
  starting transfers between devices: 24.4 us -> 12.4 us
    pallas_call x0 -> x1, Pallas kernels: none -> 371 us  [through_modes(): pl.pallas_call(functools.partial(middle, n_gx, n_gy), out_shape=(jax.Shap...]
    all_to_all x3 -> x0, blocking collectives: 224 us -> none  [the longest x1 192 us: to_cells(): lax.all_to_all(part, 'gx', split_axis=4, concat_axis=1, tiled=True)]
    dot_general x6, matrix products: 190 us -> 29.6 us  [the longest x1 13.2 us: shards(): jnp.einsum('kz,kxy->zxy', table_z, cells, precision=lax.Precision.HIGH)]
    all_to_all x4 -> x2, waiting for transfers between devices: 181 us -> 26.2 us  [swap(): lax.all_to_all(strips.reshape(devices, -1, strips.shape[1]), ('grp', 'gx'...]
    all_to_all x9 -> x0, local copies, waits for them, and re-layouts: 38.2 us -> none  [the longest x1 10.7 us: to_cells(): lax.all_to_all(lax.all_to_all(part, 'gx', split_axis=4, concat_axis=1, ti...]
    reshape x3, local copies, waits for them, and re-layouts: 19.9 us -> 1.71 us  [the longest x1 1.15 us: swap(): strips.reshape(devices, -1, strips.shape[1])]
    dot_general x1 -> x0, other arithmetic: 15.5 us -> none  [to_modes(): return jnp.einsum('ly,gzky->gzkl', table_y, part, precision=HIGH)]
    all_to_all x4 -> x2, starting transfers between devices: 24.4 us -> 12.4 us  [swap(): lax.all_to_all(strips.reshape(devices, -1, strips.shape[1]), ('grp', 'gx'...]
  transfers between devices with their start and end apart: 4 -> 2, of which waited for: 2 -> 2; matrix products, arithmetic and copies ran while one was open for 6% -> 3% of each run, Pallas kernels for 0% -> 0%
where the time goes in v1:
time: 493 us; the launch traced here: 488 us
  Pallas kernels  371 us (75%)
  local copies, waits for them, and re-layouts  43.7 us (9%)
  matrix products  29.6 us (6%)
  waiting for transfers between devices  26.2 us (5%)
  starting transfers between devices  12.4 us (3%)
    pallas_call x1, Pallas kernels, through_modes(): pl.pallas_call(functools.partial(middle, n_gx, n_gy), out_shape=(jax.Shap...  371 us
    unnamed x16, local copies, waits for them, and re-layouts  28.9 us
    all_to_all x2, waiting for transfers between devices, swap(): lax.all_to_all(strips.reshape(devices, -1, strips.shape[1]), ('grp', 'gx'...  26.2 us
    dot_general x1, matrix products, shards(): jnp.einsum('kz,kxy->zxy', table_z, cells, precision=lax.Precision.HIGH)  13.2 us
    all_to_all x2, starting transfers between devices, swap(): lax.all_to_all(strips.reshape(devices, -1, strips.shape[1]), ('grp', 'gx'...  12.4 us
    dot_general x1, matrix products, shards(): jnp.einsum('kz,zxy->kxy', table_z, forcing[0], precision=lax.Precision.HIGH)  12.1 us
  transfers between devices with their start and end apart: 2, of which 2 were waited for; matrix products, arithmetic and copies ran while one was open for 3% of the time, Pallas kernels for 0%

profile of v1, /device:TPU:9, one launch (start us, length us, event | category | flops | bytes accessed | tf_op | source)
XLA Modules:
  0.0 488.5 jit_solution(1208757930257827232)
XLA Ops:
  0.6 0.0 copy-start.2
  0.6 0.0 copy-start.4
  0.7 8.4 %copy.44 = f32[1,32,128,512]{3,2,1,0:T(8,128)} copy(f32[1,32,128,512]{3,2,1,0:T(8,128)} %param.18) | data formatting | bytes 16777216
  9.0 0.0 copy-done.4
  9.0 1.5 fusion.33
  10.5 0.3 copy.32
  10.8 0.1 rev.6
  10.9 0.0 copy-done.2
  10.9 0.6 fusion.10
  11.5 1.1 reshape.130
  12.7 0.0 copy-start.3
  12.7 6.4 %all-to-all-start = ((f32[32,4,1664]{2,1,0:T(4,128)}), f32[32,4,1664]{2,1,0:T(4,128)S(1)}, u32[]{:S(2)}, u32[]{:S(2)}) async-start(f32[32,4,1664]{2,1,0:T(4,128)} %reshape.130), calls=%async_computation | async-start | bytes 1703936 | tf_op jit(solution)/shard_map/all_to_all | solution.py:237
  19.0 0.3 copy.33
  19.3 19.8 %all-to-all-done = f32[32,4,1664]{2,1,0:T(4,128)S(1)} async-done(((f32[32,4,1664]{2,1,0:T(4,128)}), f32[32,4,1664]{2,1,0:T(4,128)S(1)}, u32[]{:S(2)}, u32[]{:S(2)}) %all-to-all-start) | async-done | bytes 852000 | tf_op jit(solution)/shard_map/all_to_all | solution.py:237
  39.2 0.3 reshape.131
  39.5 0.1 fusion.19
  39.6 0.6 convolution_subtract_fusion
  40.1 0.3 copy.22
  40.4 0.1 fusion.17
  40.5 0.1 pad_maximum_fusion
  40.6 0.5 copy.23
  41.0 1.6 reshape_reshape.3
  42.7 6.1 %all-to-all-start.1 = ((f32[32,4,1536]{2,1,0:T(4,128)}), f32[32,4,1536]{2,1,0:T(4,128)S(1)}, u32[]{:S(2)}, u32[]{:S(2)}) async-start(f32[32,4,1536]{2,1,0:T(4,128)} %reshape_reshape.3), calls=%async_computation.1 | async-start | bytes 1572864 | tf_op jit(solution)/shard_map/all_to_all | solution.py:237
  48.8 0.6 slice.100
  49.4 0.0 copy-done.3
  49.4 0.7 and_reduce_fusion
  50.1 2.6 fusion.9
  52.7 0.0 copy-start.1
  52.7 8.4 %copy.41 = f32[32,128,512]{2,1,0:T(8,128)} copy(f32[32,128,512]{2,1,0:T(8,128)} %bitcast.57) | data formatting | bytes 16777216
  61.1 6.4 %all-to-all-done.1 = f32[32,4,1536]{2,1,0:T(4,128)S(1)} async-done(((f32[32,4,1536]{2,1,0:T(4,128)}), f32[32,4,1536]{2,1,0:T(4,128)S(1)}, u32[]{:S(2)}, u32[]{:S(2)}) %all-to-all-start.1) | async-done | bytes 786464 | tf_op jit(solution)/shard_map/all_to_all | solution.py:237
  67.5 0.3 reshape.137
  67.8 0.3 copy.24
  68.0 0.6 convolution_bitcast_fusion
  68.6 3.5 fusion.15
  72.1 0.0 copy-done.1
  72.1 12.1 %fusion.2 = f32[32,128,512]{2,0,1:T(8,128)S(1)} fusion(f32[32,32,1]{1,0,2:T(8,128)S(1)} %copy-done.1, f32[32,128,512]{2,1,0:T(8,128)} %fusion.15), kind=kOutput, calls=%fused_computation.2 | convolution fusion | flops 402653184 | bytes 16781312 | tf_op jit(solution)/shard_map/kz,zxy->kxy/dot_general | solution.py:277
  84.1 8.3 %copy.26.part = f32[32,128,512]{2,1,0:T(8,128)} copy(f32[32,128,512]{2,0,1:T(8,128)S(1)} %fusion.2) | data formatting | bytes 16777216 | tf_op jit(solution)/shard_map/kz,zxy->kxy/dot_general | solution.py:277
  92.4 371.0 %middle.1 = (f32[4,512,1024]{2,1,0:T(8,128)}, f32[32,128,512]{2,1,0:T(8,128)}) custom-call(f32[32,128,512]{2,1,0:T(8,128)} %copy.26.part, f32[4,512,1024]{2,1,0:T(8,128)} %bitcast.67, f32[4,512,1024]{2,1,0:T(8,128)} %bitcast.68, bf16[2,512,512]{2,1,0:T(8,128)(2,1)} %constant.79.clone.cx, bf16[2,512,512]{2,1,0:T(8,128)(2,1)} %constant.80.clone.cxt, ...), custom_call_target="tpu_custom_call" | custom-call | flops 38654705664 | bytes 50331648 | tf_op jit(solution)/shard_map/middle/pallas_call | solution.py:200
  463.4 13.2 %fusion.4 = f32[1,32,128,512]{3,1,2,0:T(8,128)S(1)} fusion(f32[32,32,1]{1,0,2:T(8,128)S(1)} %copy-done.1, f32[32,128,512]{2,1,0:T(8,128)} %get-tuple-element.29), kind=kOutput, calls=%fused_computation.4 | convolution fusion | flops 402653184 | bytes 16781312 | tf_op jit(solution)/shard_map/kz,kxy->zxy/dot_general | solution.py:279
  476.6 0.0 copy-start
  476.6 8.3 %copy.29 = f32[1,32,128,512]{3,2,1,0:T(8,128)} copy(f32[1,32,128,512]{3,1,2,0:T(8,128)S(1)} %fusion.4) | data formatting | bytes 16777216
  484.9 0.0 copy-done
  484.9 3.4 copy.45
  (3 shorter events, 0.0 us)
Async XLA Ops:
  0.6 10.2 %copy-start.2 = (s32[1,128,1]{1,2,0:T(1,128)S(1)}, s32[1,128,1]{1,2,0:T(1,128)}, u32[]{:S(2)}) copy-start(s32[1,128,1]{1,2,0:T(1,128)} %param.19) | copy-start | bytes 1540
  0.6 8.4 %copy-start.4 = (s32[1,128,1]{1,2,0:T(1,128)S(1)}, s32[1,128,1]{1,2,0:T(1,128)}, u32[]{:S(2)}) copy-start(s32[1,128,1]{1,2,0:T(1,128)} %param.20) | copy-start | bytes 1540
  12.7 36.7 %copy-start.3 = (s32[4]{0:T(128)S(1)}, s32[4]{0:T(128)}, u32[]{:S(2)}) copy-start(s32[4]{0:T(128)} %constant.76.clone.1) | copy-start | bytes 52
  12.7 26.5 %all-to-all-start = ((f32[32,4,1664]{2,1,0:T(4,128)}), f32[32,4,1664]{2,1,0:T(4,128)S(1)}, u32[]{:S(2)}, u32[]{:S(2)}) async-start(f32[32,4,1664]{2,1,0:T(4,128)} %reshape.130), calls=%async_computation | async-start | bytes 1703936 | tf_op jit(solution)/shard_map/all_to_all | solution.py:237
  42.7 24.8 %all-to-all-start.1 = ((f32[32,4,1536]{2,1,0:T(4,128)}), f32[32,4,1536]{2,1,0:T(4,128)S(1)}, u32[]{:S(2)}, u32[]{:S(2)}) async-start(f32[32,4,1536]{2,1,0:T(4,128)} %reshape_reshape.3), calls=%async_computation.1 | async-start | bytes 1572864 | tf_op jit(solution)/shard_map/all_to_all | solution.py:237
  52.7 19.3 %copy-start.1 = (f32[32,32,1]{1,0,2:T(8,128)S(1)}, f32[32,32,1]{1,0,2:T(8,128)}, u32[]{:S(2)}) copy-start(f32[32,32,1]{1,0,2:T(8,128)} %constant.89) | copy-start | bytes 12292
  476.6 8.3 %copy-start = (f32[4,512,1024]{2,1,0:T(8,128)S(1)}, f32[4,512,1024]{2,1,0:T(8,128)}, u32[]{:S(2)}) copy-start(f32[4,512,1024]{2,1,0:T(8,128)} %get-tuple-element.28) | copy-start | bytes 25165828

commit v2 on v1

--- a/solution.py
+++ b/solution.py
@@ -38,20 +38,6 @@
         return jnp.dot(a, b, preferred_element_type=jnp.float32)
 
     return dot(left[0], right[0]) + (dot(left[0], right[1]) + dot(left[1], right[0]))
-
-
-def face_stencil(diff):
-    first = diff[..., 0, :]
-    second = diff[..., 1, :]
-    third = diff[..., 2, :]
-    return jnp.stack(
-        [
-            WEIGHTS[0] * first + WEIGHTS[1] * second + WEIGHTS[2] * third,
-            WEIGHTS[1] * first + WEIGHTS[2] * second,
-            WEIGHTS[2] * first,
-        ],
-        axis=-2,
-    )
 
 
 SERIES = tuple(float((-1) ** k * 2.0 ** (2 * k + 1) / np.prod(np.arange(1.0, 2 * k + 3))) for k in range(11))
@@ -233,6 +219,116 @@
     )
 
 
+def analyse(layers, table):
+    count = len(layers)
+    if count == 1:
+        return [layers[0] * float(table[0, 0])]
+    mid = count // 2
+    sums = [layers[m] + layers[count - 1 - m] for m in range(mid)]
+    gaps = [layers[m] - layers[count - 1 - m] for m in range(mid)]
+    modes = [None] * count
+    for k in range(1, count, 2):
+        total = gaps[0] * float(table[k, 0])
+        for m in range(1, mid):
+            total = total + gaps[m] * float(table[k, m])
+        modes[k] = total
+    modes[0::2] = analyse(sums, table[0::2, :mid])
+    return modes
+
+
+def synthesise(modes, table):
+    count = len(modes)
+    if count == 1:
+        return [modes[0] * float(table[0, 0])]
+    mid = count // 2
+    even = synthesise(modes[0::2], table[0::2, :mid])
+    layers = [None] * count
+    for m in range(mid):
+        odd = modes[1] * float(table[1, m])
+        for k in range(3, count, 2):
+            odd = odd + modes[k] * float(table[k, m])
+        layers[m] = even[m] + odd
+        layers[count - 1 - m] = even[m] - odd
+    return layers
+
+
+def tiles(ref, body):
+    rows, cols = ref.shape[1:]
+    across = cols // 128
+
+    @pl.loop(0, (rows // 8) * across)
+    def _(t):
+        row = pl.multiple_of(lax.div(t, across) * 8, 8)
+        col = pl.multiple_of(lax.rem(t, across) * 128, 128)
+        body(pl.ds(row, 8), col)
+
+
+def depth_in(table, source, low, high, part):
+    depth, _, cols_y = source.shape
+
+    def body(rows, col):
+        layers = [source[z, rows, pl.ds(col, 128)] for z in range(depth)]
+        for j in range(3):
+            at = pl.ds(pl.multiple_of(j * cols_y + col, 128), 128)
+            layers[j] = layers[j] - low[rows, at]
+            layers[depth - 1 - j] = layers[depth - 1 - j] + high[rows, at]
+        for k, mode in enumerate(analyse(layers, table)):
+            part[k, rows, pl.ds(col, 128)] = mode
+
+    tiles(source, body)
+
+
+def depth_out(table, cells, field):
+    depth = cells.shape[0]
+
+    def body(rows, col):
+        modes = [cells[k, rows, pl.ds(col, 128)] for k in range(depth)]
+        for z, layer in enumerate(synthesise(modes, table)):
+            field[z, rows, pl.ds(col, 128)] = layer
+
+    tiles(cells, body)
+
+
+def over_depth(body, table, field, *strips):
+    depth, rows_x, cols_y = field.shape
+    rows = 16
+    block = pl.BlockSpec((depth, rows, cols_y), lambda i: (0, i, 0))
+    strip = pl.BlockSpec((rows, 3 * cols_y), lambda i: (i, 0))
+    return pl.pallas_call(
+        functools.partial(body, table),
+        grid=(rows_x // rows,),
+        out_shape=jax.ShapeDtypeStruct(field.shape, jnp.float32),
+        in_specs=[block] + [strip] * len(strips),
+        out_specs=block,
+        compiler_params=pltpu.CompilerParams(vmem_limit_bytes=24 * 2**20),
+    )(field, *strips)
+
+
+def lay_faces(low0, low1, low2, high0, high1, high2, bottom, top):
+    cols_y = low0.shape[2]
+    for j, (low, high) in enumerate(((low0, high0), (low1, high1), (low2, high2))):
+        bottom[:, j * cols_y : (j + 1) * cols_y] = low[0]
+        top[:, j * cols_y : (j + 1) * cols_y] = high[0]
+
+
+def faces(pressure):
+    depth, rows_x, cols_y = pressure.shape
+
+    def layer(z):
+        return pl.BlockSpec((1, rows_x, cols_y), lambda i: (z, 0, 0))
+
+    flat = jax.ShapeDtypeStruct((rows_x, 3 * cols_y), jnp.float32)
+    whole = pl.BlockSpec((rows_x, 3 * cols_y), lambda i: (0, 0))
+    return pl.pallas_call(
+        lay_faces,
+        grid=(1,),
+        out_shape=(flat, flat),
+        in_specs=[layer(z) for z in (0, 1, 2, depth - 1, depth - 2, depth - 3)],
+        out_specs=(whole, whole),
+        compiler_params=pltpu.CompilerParams(vmem_limit_bytes=24 * 2**20),
+    )(*[pressure] * 6)
+
+
 def swap(strips, devices):
     return lax.all_to_all(
         strips.reshape(devices, -1, strips.shape[1]),
@@ -249,12 +345,10 @@
     cols_y = source.shape[3]
     long_x = modes_now.shape[2]
     long_y = modes_now.shape[3]
-    table_z = jnp.asarray(cosine_table(depth))
+    table_z = cosine_table(depth)
     table_x = cosine_table(long_x)
     table_y = cosine_table(long_y)
-    layers = pressure_now[0]
-    top = jnp.transpose(layers[depth - 3 :][::-1], (1, 0, 2)).reshape(rows_x, 3 * cols_y)
-    bottom = jnp.transpose(layers[0:3], (1, 0, 2)).reshape(rows_x, 3 * cols_y)
+    bottom, top = faces(pressure_now[0])
     devices = lax.axis_size(("grp", "gx", "gy"))
     slots_per = max(2, rows_x // devices)
     slots = strip_slot.reshape(-1)
@@ -267,16 +361,22 @@
     marks = rims[:, 3 * cols_y].astype(jnp.int32) - 1
     meet = (marks[:, None] == jnp.arange(rows_x, dtype=jnp.int32)[None, :]).astype(jnp.float32)
     met = jnp.dot(meet, bottom, precision=HIGH)
-    diff = (met - rims[:, : 3 * cols_y]).reshape(-1, 3, cols_y)
-    force = face_stencil(diff).reshape(-1, 3 * cols_y)
+    diff = met - rims[:, : 3 * cols_y]
+    first, second, third = (diff[:, j * cols_y : (j + 1) * cols_y] for j in range(3))
+    force = jnp.concatenate(
+        [
+            WEIGHTS[0] * first + WEIGHTS[1] * second + WEIGHTS[2] * third,
+            WEIGHTS[1] * first + WEIGHTS[2] * second,
+            WEIGHTS[2] * first,
+        ],
+        axis=1,
+    )
     back = swap(force, devices)
-    bottom_force = -jnp.dot(meet.T, force, precision=HIGH).reshape(rows_x, 3, cols_y)
-    top_force = jnp.dot(put.T, back, precision=HIGH).reshape(rows_x, 3, cols_y)
-    forcing = source.at[0, 0:3].add(jnp.transpose(bottom_force, (1, 0, 2)))
-    forcing = forcing.at[0, depth - 3 :].add(jnp.transpose(top_force, (1, 0, 2))[::-1])
-    part = jnp.einsum("kz,zxy->kxy", table_z, forcing[0], precision=lax.Precision.HIGH)
+    bottom_force = jnp.dot(meet.T, force, precision=HIGH)
+    top_force = jnp.dot(put.T, back, precision=HIGH)
+    part = over_depth(depth_in, table_z, source[0], bottom_force, top_force)
     modes_new, cells = through_modes(part, modes_now[0], modes_old[0], table_x, table_y)
-    pressure_next = jnp.einsum("kz,kxy->zxy", table_z, cells, precision=lax.Precision.HIGH)
+    pressure_next = over_depth(depth_out, table_z, cells)
     return (modes_new[None], pressure_next[None])
 
 

time: 493 us -> 463 us (0.939)
  matrix products: 29.6 us -> 2.28 us
  blocking collectives: 0 us -> 26.3 us
  local copies, waits for them, and re-layouts: 43.7 us -> 19.4 us
  Pallas kernels: 371 us -> 389 us
  waiting for transfers between devices: 26.2 us -> 18.3 us
  starting transfers between devices: 12.4 us -> 5.81 us
    dot_general x4 -> x2, matrix products: 28.4 us -> 1.13 us  [the longest x1 0.58 us: shards(): bottom_force = jnp.dot(meet.T, force, precision=HIGH)]
    all_to_all x0 -> x1, blocking collectives: none -> 26.3 us  [swap(): lax.all_to_all(strips.reshape(devices, -1, strips.shape[1]), ('grp', 'gx'...]
    pallas_call x0 -> x3, Pallas kernels: none -> 18.2 us  [the longest x2 18.1 us: over_depth(): pl.pallas_call(functools.partial(body, table), grid=(rows_x // rows,), ou...]
    unnamed x16 -> x13, local copies, waits for them, and re-layouts: 28.9 us -> 17.4 us
    dot_general x2 -> x0, local copies, waits for them, and re-layouts: 8.51 us -> none  [the longest x1 8.25 us: shards(): jnp.einsum('kz,zxy->kxy', table_z, forcing[0], precision=lax.Precision.HIGH)]
    all_to_all x2 -> x1, waiting for transfers between devices: 26.2 us -> 18.3 us  [swap(): lax.all_to_all(strips.reshape(devices, -1, strips.shape[1]), ('grp', 'gx'...]
    all_to_all x2 -> x1, starting transfers between devices: 12.4 us -> 5.81 us  [swap(): lax.all_to_all(strips.reshape(devices, -1, strips.shape[1]), ('grp', 'gx'...]
  transfers between devices with their start and end apart: 2 -> 1, of which waited for: 2 -> 1; matrix products, arithmetic and copies ran while one was open for 3% -> 0% of each run, Pallas kernels for 0% -> 0%
where the time goes in v2:
time: 463 us
  Pallas kernels  389 us (84%)
  blocking collectives  26.3 us (6%)
  local copies, waits for them, and re-layouts  19.4 us (4%)
  waiting for transfers between devices  18.3 us (4%)
  starting transfers between devices  5.81 us (1%)
    pallas_call x1, Pallas kernels, through_modes(): pl.pallas_call(functools.partial(middle, n_gx, n_gy), out_shape=(jax.Shap...  371 us
    all_to_all x1, blocking collectives, swap(): lax.all_to_all(strips.reshape(devices, -1, strips.shape[1]), ('grp', 'gx'...  26.3 us
    all_to_all x1, waiting for transfers between devices, swap(): lax.all_to_all(strips.reshape(devices, -1, strips.shape[1]), ('grp', 'gx'...  18.3 us
    pallas_call x2, Pallas kernels, over_depth(): pl.pallas_call(functools.partial(body, table), grid=(rows_x // rows,), ou...  18.1 us
    unnamed x13, local copies, waits for them, and re-layouts  17.4 us
  transfers between devices with their start and end apart: 1, of which 1 were waited for; matrix products, arithmetic and copies ran while one was open for 0% of the time, Pallas kernels for 0%

profile of v2, /device:TPU:9, one launch (start us, length us, event | category | flops | bytes accessed | tf_op | source)
XLA Modules:
  0.0 463.0 jit_solution(6901159932704680700)
XLA Ops:
  0.6 0.7 convert_bitcast_fusion
  1.3 0.0 copy-start
  1.3 3.4 copy-done
  4.7 0.0 copy-start.5
  4.7 0.1 shard_map.113
  4.8 0.1 broadcast_in_dim.6
  4.9 0.5 copy-done.5
  5.3 0.6 fusion
  5.9 0.2 reshape.27
  6.2 26.3 %all_to_all.10 = f32[32,4,1664]{2,1,0:T(4,128)S(1)} all-to-all(f32[32,4,1664]{2,1,0:T(4,128)S(1)} %reshape.27), channel_id=1, replica_groups=mesh['grp'=4,'gx'=4,'gy'=2] {'grp','gx','gy'}, dimensions={0} | all-to-all | bytes 1703936 | tf_op jit(solution)/shard_map/all_to_all | solution.py:333
  32.4 0.3 reshape.28
  32.7 0.1 fusion.6
  32.8 0.6 convolution_subtract_fusion
  33.4 0.1 fusion.4
  33.6 0.1 pad_maximum_fusion
  33.6 1.1 reshape.29
  34.7 5.8 %all-to-all-start.1 = ((f32[32,4,1536]{2,1,0:T(4,128)}), f32[32,4,1536]{2,1,0:T(4,128)S(1)}, u32[]{:S(2)}, u32[]{:S(2)}) async-start(f32[32,4,1536]{2,1,0:T(4,128)} %reshape.29), calls=%async_computation.1 | async-start | bytes 1572864 | tf_op jit(solution)/shard_map/all_to_all | solution.py:333
  40.5 0.6 fusion.7.low
  41.1 18.3 %all-to-all-done.1 = f32[32,4,1536]{2,1,0:T(4,128)S(1)} async-done(((f32[32,4,1536]{2,1,0:T(4,128)}), f32[32,4,1536]{2,1,0:T(4,128)S(1)}, u32[]{:S(2)}, u32[]{:S(2)}) %all-to-all-start.1) | async-done | bytes 786464 | tf_op jit(solution)/shard_map/all_to_all | solution.py:333
  59.4 0.3 reshape.30
  59.7 0.6 fusion.8.high
  60.2 0.0 copy-start.1
  60.2 3.4 copy-done.1
  63.6 9.3 %shard_map.114.part = f32[32,128,512]{2,1,0:T(8,128)S(1)} custom-call(f32[32,128,512]{2,1,0:T(8,128)S(1)} %bitcast.17, f32[128,1536]{1,0:T(8,128)S(1)} %fusion.7.low, f32[128,1536]{1,0:T(8,128)S(1)} %fusion.8.high), custom_call_target="tpu_custom_call" | custom-call | tf_op jit(solution)/shard_map/pallas_call | solution.py:297
  72.9 0.0 copy-start.2
  73.0 3.4 copy-done.2
  76.3 371.0 %middle.1 = (f32[4,512,1024]{2,1,0:T(8,128)}, f32[32,128,512]{2,1,0:T(8,128)}) custom-call(f32[32,128,512]{2,1,0:T(8,128)} %copy-done.2, f32[4,512,1024]{2,1,0:T(8,128)} %bitcast.22, f32[4,512,1024]{2,1,0:T(8,128)} %bitcast.23, bf16[2,512,512]{2,1,0:T(8,128)(2,1)} %constant.18.clone.cx, bf16[2,512,512]{2,1,0:T(8,128)(2,1)} %constant.19.clone.cxt, ...), custom_call_target="tpu_custom_call" | custom-call | flops 38654705664 | bytes 50331648 | tf_op jit(solution)/shard_map/middle/pallas_call | solution.py:186
  447.4 0.0 copy-start.3
  447.4 3.4 copy-done.3
  450.8 0.0 copy-start.4
  450.8 8.8 %shard_map.115 = f32[32,128,512]{2,1,0:T(8,128)} custom-call(f32[32,128,512]{2,1,0:T(8,128)S(1)} %copy-done.3), custom_call_target="tpu_custom_call" | custom-call | tf_op jit(solution)/shard_map/pallas_call | solution.py:297
  459.6 0.0 copy-done.4
  459.6 3.4 copy.13
Async XLA Ops:
  1.3 3.4 copy-start
  4.7 0.7 copy-start.5
  34.7 24.7 %all-to-all-start.1 = ((f32[32,4,1536]{2,1,0:T(4,128)}), f32[32,4,1536]{2,1,0:T(4,128)S(1)}, u32[]{:S(2)}, u32[]{:S(2)}) async-start(f32[32,4,1536]{2,1,0:T(4,128)} %reshape.29), calls=%async_computation.1 | async-start | bytes 1572864 | tf_op jit(solution)/shard_map/all_to_all | solution.py:333
  60.2 3.4 copy-start.1
  72.9 3.4 copy-start.2
  447.4 3.4 copy-start.3
  450.8 8.8 %copy-start.4 = (f32[4,512,1024]{2,1,0:T(8,128)S(1)}, f32[4,512,1024]{2,1,0:T(8,128)}, u32[]{:S(2)}) copy-start(f32[4,512,1024]{2,1,0:T(8,128)} %get-tuple-element.8) | copy-start | bytes 25165828
